TPU v7x, 32 devices: a whole 2x2x4 slice. The times are simulated.
32 devices in a mesh: branch: 4 (over z), vocab: 8 (over y, x, core).
Axes of the slice: x: 2, y: 2, z: 4, core: 2. Of those that a mesh axis runs over, the one named last changes fastest.
Arguments:
- teacher_hidden: bfloat16 [4, 768, 4096], P('branch', None, 'vocab'), may hold values from -300 to 300
- teacher_weight: bfloat16 [4, 4096, 32000], P('branch', None, 'vocab'), may hold values from -0.375 to 0.375
- student_hidden: bfloat16 [768, 4096], P('branch', 'vocab'), may hold values from -300 to 300
- student_weight: bfloat16 [4096, 32000], P(None, 'vocab'), may hold values from -0.375 to 0.375
- branch_weight: float32 [4], replicated, may hold values from 0.2 to 5
- assignment: int32 [4], replicated, may hold values from 0 to 3, each once
- targets: int32 [768], P('branch'), may hold values from 0 to 31999
Outputs:
- divergence: float32 [768], P('branch')
- target_loss: float32 [768], P('branch')
Inputs may be any that keep to these rules, and one draw needn't show every extreme that they name: `assignment`: each branch number appears once.
All inputs are finite; a program needn't handle non-finite values.
Results may differ from a plain program's by a relative error of at most 0.0003.
Values may be sent and summed in bfloat16 or wider, within the bound.
A program may use at most 192 MiB of HBM per device.

v0:
```python
import jax
import jax.numpy as jnp
from jax import lax
from jax.sharding import PartitionSpec as P


def vocab_total(logits):
    local_max = jnp.max(logits, axis=1)
    highest = lax.pmax(local_max, "vocab")
    summed = lax.psum(jnp.sum(jnp.exp(logits - highest[:, None]), axis=1), "vocab")
    return highest + jnp.log(summed)


def add_product(piece, weights):
    return jnp.dot(piece, weights, preferred_element_type=jnp.float32)


def per_device(
    teacher_hidden,
    teacher_weight,
    student_hidden,
    student_weight,
    branch_weight,
    assignment,
    targets,
):
    hidden_rows = teacher_hidden[0]
    weights = teacher_weight[0]
    width_shard = weights.shape[1]
    group = lax.axis_index("branch")
    share = branch_weight / jnp.sum(branch_weight)
    log_share = jnp.log(share)[assignment]
    own_share = jnp.sum(jnp.where(jnp.arange(log_share.shape[0]) == group, log_share, 0.0))
    teacher_logits = add_product(lax.all_gather(hidden_rows, "vocab", axis=1, tiled=True), weights)
    shifted = teacher_logits - vocab_total(teacher_logits)[:, None] + own_share
    gathered = lax.all_to_all(shifted[None], "branch", split_axis=1, concat_axis=0, tiled=True)
    highest = jnp.max(gathered, axis=0)
    mixture = highest + jnp.log(jnp.sum(jnp.exp(gathered - highest[None]), axis=0))
    student_logits = add_product(
        lax.all_gather(student_hidden, "vocab", axis=1, tiled=True), student_weight
    )
    log_student = student_logits - vocab_total(student_logits)[:, None]
    columns = lax.axis_index("vocab") * width_shard + jnp.arange(width_shard, dtype=jnp.int32)
    matches = columns[None, :] == targets[:, None]
    kl_terms = jnp.sum(jnp.exp(mixture) * (mixture - log_student), axis=1)
    target_terms = -jnp.sum(jnp.where(matches, log_student, 0.0), axis=1)
    divergence, target_loss = lax.psum((kl_terms, target_terms), "vocab")
    return (divergence, target_loss)


def solution(mesh):
    in_specs = (
        P("branch", None, "vocab"),
        P("branch", None, "vocab"),
        P("branch", "vocab"),
        P(None, "vocab"),
        P(),
        P(),
        P("branch"),
    )
    out_specs = (P("branch"), P("branch"))
    return jax.shard_map(
        per_device, mesh=mesh, in_specs=in_specs, out_specs=out_specs, check_vma=False
    )
```

profile of v0, /device:TPU:0, one launch (start us, length us, event | category | flops | bytes accessed | tf_op | source)
XLA Modules:
  0.0 530.9 jit_solution(16949012237943365345)
XLA Ops:
  7.2 0.0 all-gather.4.cloned.1.call-start
  7.2 0.7 all-gather.4.cloned.1.call-update
  7.9 0.0 all-gather.6.cloned.1.call-start
  7.9 0.7 all-gather.6.cloned.1.call-update
  8.7 1.3 reduce_sum.64
  9.9 0.7 compare_select_fusion
  10.6 1.3 divide_log_fusion
  11.9 0.6 gather_fusion
  12.5 0.6 fusion.3
  13.1 25.3 %all-gather.4.cloned.1.call-done = bf16[192,4096]{1,0:T(8,128)(2,1)} async-done(((bf16[192,512]{1,0:T(8,128)(2,1)}), bf16[192,4096]{1,0:T(8,128)(2,1)}) %all-gather.4.cloned.1.call-update) | async-done | bytes 1572880 | tf_op jit(solution)/shard_map/all_gather | solution.py:40
  38.5 17.0 %fusion.4 = (f32[192]{0:T(256)S(1)}, f32[192,4000]{1,0:T(8,128)S(1)}) fusion(bf16[192,4096]{1,0:T(8,128)(2,1)} %all-gather.4.cloned.1.call-done, bf16[4096,4000]{0,1:T(8,128)(2,1)} %param.10), kind=kOutput, calls=%fused_computation.18 | convolution fusion | flops 6292224000 | bytes 37413632 | tf_op jit(solution)/shard_map/dot_general | solution.py:15
  55.5 0.0 copy-start
  55.5 31.6 %all-gather.6.cloned.1.call-done = bf16[1,768,4096]{2,1,0:T(8,128)(2,1)} async-done(((bf16[1,768,512]{2,1,0:T(8,128)(2,1)}), bf16[1,768,4096]{2,1,0:T(8,128)(2,1)}) %all-gather.6.cloned.1.call-update) | async-done | bytes 6291472 | tf_op jit(solution)/shard_map/all_gather | solution.py:34
  87.1 32.5 %fusion.5 = (f32[768]{0:T(1024)S(1)}, f32[768,4000]{0,1:T(8,128)}) fusion(bf16[1,4096,4000]{1,2,0:T(8,128)(2,1)} %param.8, bf16[1,768,4096]{2,1,0:T(8,128)(2,1)} %all-gather.6.cloned.1.call-done), kind=kOutput, calls=%fused_computation.19 | convolution fusion | flops 25168896000 | bytes 51350528 | tf_op jit(solution)/shard_map/dot_general | solution.py:15
  119.6 13.3 %all-reduce.2 = (f32[192]{0:T(256)S(1)}, f32[768]{0:T(1024)S(1)}) all-reduce(f32[192]{0:T(256)S(1)} %get-tuple-element.10, f32[768]{0:T(1024)S(1)} %get-tuple-element.12), channel_id=1, replica_groups=mesh['branch'=4,'vocab'=8] {'vocab'}, use_global_device_ids=true, to_apply=%region_9.10 | all-reduce | flops 960 | bytes 7680 | tf_op jit(solution)/shard_map/pmax | solution.py:9
  132.9 6.2 %exponential_reduce_fusion.1 = f32[768]{0:T(1024)S(1)} fusion(f32[768,4000]{0,1:T(8,128)} %get-tuple-element.13, f32[768]{0:T(1024)S(1)} %get-tuple-element.9), kind=kLoop, calls=%fused_computation.5 | loop fusion | flops 6143232 | bytes 12294144 | tf_op jit(solution)/shard_map/reduce_sum | solution.py:10
  139.1 0.0 copy-done
  139.1 0.6 exponential_reduce_fusion.2
  139.7 12.0 %all-reduce.1 = (f32[192]{0:T(256)S(1)}, f32[768]{0:T(1024)S(1)}) all-reduce(f32[192]{0:T(256)S(1)} %exponential_reduce_fusion.2, f32[768]{0:T(1024)S(1)} %exponential_reduce_fusion.1), channel_id=1, replica_groups=mesh['branch'=4,'vocab'=8] {'vocab'}, use_global_device_ids=true, to_apply=%region_11.12 | all-reduce | flops 960 | bytes 7680 | tf_op jit(solution)/shard_map/psum | solution.py:10
  151.7 10.6 %add_bitcast_fusion = f32[1,768,4000]{1,2,0:T(8,128)} fusion(f32[768,4000]{0,1:T(8,128)} %get-tuple-element.13, f32[]{:T(128)} %fusion.3, f32[768]{0:T(1024)S(1)} %log_add_fusion), kind=kLoop, calls=%fused_computation.4 | loop fusion | flops 6144000 | bytes 24579076 | tf_op jit(solution)/shard_map/broadcast_in_dim | solution.py:36
  162.3 28.3 %copy.11 = f32[1,768,4000]{2,0,1:T(1,128)} copy(f32[1,768,4000]{1,2,0:T(8,128)} %add_bitcast_fusion) | data formatting | bytes 24576000 | tf_op jit(solution)/shard_map/broadcast_in_dim | solution.py:36
  190.5 6.5 %all-to-all-start = ((f32[1,768,4000]{2,0,1:T(1,128)}), f32[1,768,4000]{2,0,1:T(1,128)}, u32[]{:S(2)}, u32[]{:S(2)}) async-start(f32[1,768,4000]{2,0,1:T(1,128)} %copy.11), calls=%async_computation | async-start | bytes 25165824 | tf_op jit(solution)/shard_map/all_to_all | solution.py:36
  197.1 273.0 %all-to-all-done = f32[1,768,4000]{2,0,1:T(1,128)} async-done(((f32[1,768,4000]{2,0,1:T(1,128)}), f32[1,768,4000]{2,0,1:T(1,128)}, u32[]{:S(2)}, u32[]{:S(2)}) %all-to-all-start) | async-done | bytes 12288032 | tf_op jit(solution)/shard_map/all_to_all | solution.py:36
  470.1 21.7 %copy.12 = f32[1,768,4000]{2,1,0:T(8,128)} copy(f32[1,768,4000]{2,0,1:T(1,128)} %all-to-all-done) | data formatting | bytes 24576000
  491.8 6.2 %reduce_max.28 = f32[192,4000]{1,0:T(8,128)S(1)} reduce(f32[4,192,4000]{2,1,0:T(8,128)} %bitcast.15, f32[]{:T(128)} %constant.7.clone.1), dimensions={0}, to_apply=%region_6.7 | reduce | flops 2304000 | bytes 15360004 | tf_op jit(solution)/shard_map/reduce_max | solution.py:37
  498.0 0.0 copy-start.1
  498.0 9.4 %exponential_reduce_fusion = f32[192,4000]{1,0:T(8,128)} fusion(f32[4,192,4000]{2,1,0:T(8,128)} %bitcast.16, f32[192,4000]{1,0:T(8,128)S(1)} %reduce_max.28), kind=kLoop, calls=%fused_computation.3 | loop fusion | flops 5376000 | bytes 18432000 | tf_op jit(solution)/shard_map/reduce_sum | solution.py:38
  507.3 0.0 copy-done.1
  507.4 4.3 select_reduce_fusion
  511.7 12.4 %all-reduce = (f32[192]{0:T(256)}, f32[192]{0:T(256)}) all-reduce(f32[192]{0:T(256)S(1)} %get-tuple-element.3, f32[192]{0:T(256)S(1)} %neg.3), channel_id=1, replica_groups=mesh['branch'=4,'vocab'=8] {'vocab'}, use_global_device_ids=true, to_apply=%region_13.14 | all-reduce | flops 384 | bytes 3072 | tf_op jit(solution)/shard_map/psum | solution.py:47
  (5 shorter events, 0.0 us)
Async XLA Ops:
  7.2 31.3 %all-gather.4.cloned.1.call-start = ((), (), s32[]{:S(2)}) async-start(), calls=%async_computation.1 | async-start | bytes 1769472 | tf_op jit(solution)/shard_map/all_gather | solution.py:40
  7.9 79.2 %all-gather.6.cloned.1.call-start = ((), (), s32[]{:S(2)}) async-start(), calls=%async_computation.2 | async-start | bytes 7077888 | tf_op jit(solution)/shard_map/all_gather | solution.py:34
  55.5 83.6 %copy-start = (f32[192,4000]{1,0:T(8,128)}, f32[192,4000]{1,0:T(8,128)S(1)}, u32[]{:S(2)}) copy-start(f32[192,4000]{1,0:T(8,128)S(1)} %get-tuple-element.11) | copy-start | bytes 9216004
  190.5 279.6 %all-to-all-start = ((f32[1,768,4000]{2,0,1:T(1,128)}), f32[1,768,4000]{2,0,1:T(1,128)}, u32[]{:S(2)}, u32[]{:S(2)}) async-start(f32[1,768,4000]{2,0,1:T(1,128)} %copy.11), calls=%async_computation | async-start | bytes 25165824 | tf_op jit(solution)/shard_map/all_to_all | solution.py:36
  498.0 9.4 %copy-start.1 = (s32[192]{0:T(256)S(1)}, s32[192]{0:T(256)}, u32[]{:S(2)}) copy-start(s32[192]{0:T(256)} %param.13) | copy-start | bytes 2308
Sparse Core Ops, SparseCore 0:
  9.9 28.5 all-gather.3
  40.4 46.6 all-gather.5
where the time goes:
time: 532 us; the launch traced here: 531 us
  waiting for transfers between devices  331 us (62%)
  local copies, waits for them, and re-layouts  50.6 us (10%)
  matrix products  49.5 us (9%)
  other arithmetic  41 us (8%)
  blocking collectives  37.7 us (7%)
  between operations  14.1 us (3%)
  starting transfers between devices  6.59 us (1%)
    all_to_all x1, waiting for transfers between devices, per_device(): lax.all_to_all(shifted[None], 'branch', split_axis=1, concat_axis=0, tile...  273 us
    dot_general x2, matrix products, add_product(): return jnp.dot(piece, weights, preferred_element_type=jnp.float32)  49.5 us
    all_gather x1, waiting for transfers between devices, per_device(): lax.all_gather(hidden_rows, 'vocab', axis=1, tiled=True)  31.6 us
    broadcast_in_dim x1, local copies, waits for them, and re-layouts, per_device(): shifted[None]  28.3 us
    all_gather x1, waiting for transfers between devices, per_device(): lax.all_gather(student_hidden, 'vocab', axis=1, tiled=True)  25.3 us
    unnamed x5, local copies, waits for them, and re-layouts  21.7 us
    pmax x1, blocking collectives, vocab_total(): highest = lax.pmax(local_max, 'vocab')  13.3 us
    psum x1, blocking collectives, per_device(): divergence, target_loss = lax.psum((kl_terms, target_terms), 'vocab')  12.4 us
  transfers between devices with their start and end apart: 3, of which 3 were waited for; matrix products, arithmetic and copies ran while one was open for 4% of the time, Pallas kernels for 0%

commit v1 on v0

v1 whole, which is shorter than its diff:
```python
import jax
import jax.numpy as jnp
from jax import lax
from jax.sharding import PartitionSpec as P

CHUNKS = 6
SCALE = 2.0**30


def encode(p):
    p = p * SCALE
    p = p * p
    return (p * p).astype(jnp.bfloat16)


def decode(code):
    return lax.rsqrt(lax.rsqrt(code.astype(jnp.float32))) * (1.0 / SCALE)


def add_product(piece, weights):
    return jnp.dot(piece, weights, preferred_element_type=jnp.float32)


def max_and_sum(logits):
    top = jnp.max(logits, axis=1)
    return top, jnp.sum(jnp.exp(logits - top[:, None]), axis=1)


def merge_lse(tops, sums):
    top = jnp.max(tops, axis=0)
    return top + jnp.log(jnp.sum(sums * jnp.exp(tops - top[None]), axis=0))


def per_device(
    teacher_hidden,
    teacher_weight,
    student_hidden,
    student_weight,
    branch_weight,
    assignment,
    targets,
):
    weights = teacher_weight[0]
    width = weights.shape[1]
    group = lax.axis_index("branch")
    n = lax.axis_size("branch")
    half_n = n // 2
    tokens = teacher_hidden.shape[1]
    half = tokens // 2
    rows = half // CHUNKS
    share = branch_weight / jnp.sum(branch_weight)
    log_share = jnp.log(share)[assignment]
    own_share = jnp.sum(jnp.where(jnp.arange(n) == group, log_share, 0.0))

    hidden = lax.all_gather(teacher_hidden[0], "vocab", axis=1, tiled=True)
    groups = [list(range(half_n)), list(range(half_n, n))]
    student = lax.all_gather(student_hidden, "branch", axis=0, tiled=True, axis_index_groups=groups)
    picks = lax.all_gather(targets, "branch", axis=0, tiled=True, axis_index_groups=groups)
    student = lax.all_gather(student, "vocab", axis=1, tiled=True)

    logits = add_product(hidden, weights)
    top, total = max_and_sum(logits)
    parts = lax.all_gather(jnp.stack([top, total]), "vocab", axis=0)
    lse = merge_lse(parts[:, 0], parts[:, 1])
    offset = own_share - lse

    student_logits = add_product(student, student_weight)

    def own(first, chunk):
        start = first + jnp.clip(chunk, 0, CHUNKS - 1) * rows
        piece = lax.dynamic_slice(logits, (start, 0), (rows, width))
        return jnp.exp(piece + lax.dynamic_slice(offset, (start,), (rows,))[:, None])

    up = [(i, i + 1) for i in range(n - 1)]
    down = [(i + 1, i) for i in range(n - 1)]
    from_left = jnp.zeros((rows, width), jnp.bfloat16)
    from_right = from_left
    last = group == n - 1
    ends = []
    for step in range(CHUNKS + n - 1):
        up_sum = own(half, step - group) + decode(from_left)
        down_sum = own(0, step - (n - 1 - group)) + decode(from_right)
        if step >= n - 1:
            ends.append(jnp.where(last, up_sum, down_sum))
        if step < CHUNKS + n - 2:
            from_left = lax.ppermute(encode(up_sum), "branch", up)
            from_right = lax.ppermute(encode(down_sum), "branch", down)
    q = jnp.concatenate(ends, axis=0)
    mixture = jnp.log(jnp.maximum(q, 1e-37))
    s_top, s_total = max_and_sum(student_logits)
    shifted = student_logits - s_top[:, None]
    columns = lax.axis_index("vocab") * width + jnp.arange(width, dtype=jnp.int32)
    matches = columns[None, :] == picks[:, None]
    hit = jnp.sum(jnp.where(matches, student_logits, 0.0), axis=1)
    cross = jnp.sum(q * (mixture - shifted), axis=1)
    mass = jnp.sum(q, axis=1)
    parts = lax.all_gather(jnp.stack([s_top, s_total, hit, cross, mass]), "vocab", axis=0)
    s_lse = merge_lse(parts[:, 0], parts[:, 1])
    loss = s_lse - jnp.sum(parts[:, 2], axis=0)
    mass = jnp.sum(parts[:, 4], axis=0)
    cross = jnp.sum(parts[:, 3] + parts[:, 4] * (s_lse[None] - parts[:, 0]), axis=0)
    divergence = cross / mass - jnp.log(mass)
    both = lax.all_gather(jnp.stack([divergence, loss]), "branch", axis=0)
    mine = jnp.where(group < half_n, both[0], both[n - 1])
    per = tokens // n
    mine = lax.dynamic_slice(mine, (0, (group % half_n) * per), (2, per))
    return mine[0], mine[1]


def solution(mesh):
    in_specs = (
        P("branch", None, "vocab"),
        P("branch", None, "vocab"),
        P("branch", "vocab"),
        P(None, "vocab"),
        P(),
        P(),
        P("branch"),
    )
    out_specs = (P("branch"), P("branch"))
    return jax.shard_map(
        per_device, mesh=mesh, in_specs=in_specs, out_specs=out_specs, check_vma=False
    )
```

time: 532 us -> 373 us (0.70)
  waiting for transfers between devices: 331 us -> 74.3 us
  local copies, waits for them, and re-layouts: 50.6 us -> 89.4 us
  starting transfers between devices: 6.59 us -> 38.2 us
  blocking collectives: 37.7 us -> 55 us
    all_to_all x1 -> x0, waiting for transfers between devices: 273 us -> none  [per_device(): lax.all_to_all(shifted[None], 'branch', split_axis=1, concat_axis=0, tile...]
    all_gather x0 -> x4, blocking collectives: none -> 46.4 us  [the longest x1 16 us: per_device(): lax.all_gather(student_hidden, 'branch', axis=0, tiled=True, axis_index_g...]
    ppermute x0 -> x16, starting transfers between devices: none -> 38.2 us  [the longest x8 27.7 us: per_device(): from_left = lax.ppermute(encode(up_sum), 'branch', up)]
    unnamed x5 -> x31, local copies, waits for them, and re-layouts: 21.7 us -> 52.6 us
    dynamic_slice x0 -> x2, local copies, waits for them, and re-layouts: none -> 29 us  [the longest x1 28.8 us: own(): piece = lax.dynamic_slice(logits, (start, 0), (rows, width))]
    convert_element_type x0 -> x11, other arithmetic: none -> 28.3 us  [encode(): return (p * p).astype(jnp.bfloat16)]
    broadcast_in_dim x1 -> x0, local copies, waits for them, and re-layouts: 28.3 us -> none  [per_device(): shifted[None]]
    ppermute x0 -> x16, waiting for transfers between devices: none -> 26.8 us  [the longest x8 19.7 us: per_device(): from_right = lax.ppermute(encode(down_sum), 'branch', down)]
  transfers between devices with their start and end apart: 3 -> 18, of which waited for: 3 -> 9; matrix products, arithmetic and copies ran while one was open for 4% -> 28% of each run, Pallas kernels for 0% -> 0%
where the time goes in v1:
time: 373 us; the launch traced here: 371 us
  local copies, waits for them, and re-layouts  89.4 us (24%)
  waiting for transfers between devices  74.3 us (20%)
  blocking collectives  55 us (15%)
  matrix products  54.7 us (15%)
  other arithmetic  44.4 us (12%)
  starting transfers between devices  38.2 us (10%)
  between operations  15.1 us (4%)
    dot_general x2, matrix products, add_product(): return jnp.dot(piece, weights, preferred_element_type=jnp.float32)  54.7 us
    unnamed x31, local copies, waits for them, and re-layouts  52.6 us
    all_gather x1, waiting for transfers between devices, per_device(): hidden = lax.all_gather(teacher_hidden[0], 'vocab', axis=1, tiled=True)  46.8 us
    dynamic_slice x1, local copies, waits for them, and re-layouts, own(): piece = lax.dynamic_slice(logits, (start, 0), (rows, width))  28.8 us
    convert_element_type x11, other arithmetic, encode(): return (p * p).astype(jnp.bfloat16)  28.3 us
    ppermute x8, starting transfers between devices, per_device(): from_left = lax.ppermute(encode(up_sum), 'branch', up)  27.7 us
    ppermute x8, waiting for transfers between devices, per_device(): from_right = lax.ppermute(encode(down_sum), 'branch', down)  19.7 us
    all_gather x1, blocking collectives, per_device(): lax.all_gather(student_hidden, 'branch', axis=0, tiled=True, axis_index_g...  16 us
  transfers between devices with their start and end apart: 18, of which 9 were waited for; matrix products, arithmetic and copies ran while one was open for 28% of the time, Pallas kernels for 0%

profile of v1, /device:TPU:0, one launch (start us, length us, event | category | flops | bytes accessed | tf_op | source)
XLA Modules:
  0.0 371.2 jit_solution(1153633671413283369)
XLA Ops:
  12.5 46.8 %all-gather.12.cloned.1.call-done = bf16[1,768,4096]{2,1,0:T(8,128)(2,1)} async-done(((bf16[1,768,512]{2,1,0:T(8,128)(2,1)}), bf16[1,768,4096]{2,1,0:T(8,128)(2,1)}) %all-gather.12.cloned.1.call-update) | async-done | bytes 6291472 | tf_op jit(solution)/shard_map/all_gather | solution.py:55
  59.3 31.4 %fusion.18 = (f32[768]{0:T(1024)S(1)}, f32[768,4000]{0,1:T(8,128)S(1)}) fusion(bf16[1,4096,4000]{1,2,0:T(8,128)(2,1)} %param.8, bf16[1,768,4096]{2,1,0:T(8,128)(2,1)} %all-gather.12.cloned.1.call-done), kind=kOutput, calls=%fused_computation.95 | convolution fusion | flops 25168896000 | bytes 51350528 | tf_op jit(solution)/shard_map/dot_general | solution.py:21
  90.7 4.5 %copy-done = f32[768,4000]{0,1:T(8,128)} copy-done((f32[768,4000]{0,1:T(8,128)}, f32[768,4000]{0,1:T(8,128)S(1)}, u32[]{:S(2)}) %copy-start) | copy-done | bytes 12288024
  96.9 9.1 %all-gather.4 = f32[8,2,768]{2,1,0:T(2,128)S(1)} all-gather(f32[1,2,768]{2,1,0:T(2,128)S(1)} %maximum_bitcast_fusion), channel_id=3, replica_groups=mesh['branch'=4,'vocab'=8] {'vocab'}, dimensions={0}, use_global_device_ids=true | all-gather | bytes 55296 | tf_op jit(solution)/shard_map/all_gather | solution.py:63
  106.7 28.8 %constant_dynamic-slice_fusion.3 = (f32[64,4000]{0,1:T(8,128)}, f32[64,4000]{0,1:T(8,128)}, f32[64,4000]{0,1:T(8,128)}, f32[64,4000]{0,1:T(8,128)}, f32[64,4000]...) fusion(f32[768,4000]{0,1:T(8,128)} %copy-done, ...), kind=kLoop, calls=%fused_computation.59 | loop fusion | bytes 36864072 | tf_op jit(solution)/shard_map/dynamic_slice | solution.py:71
  139.0 3.8 %collective-permute-start = (bf16[64,4000]{1,0:T(8,128)(2,1)}, bf16[64,4000]{1,0:T(8,128)(2,1)}, u32[]{:S(2)}, u32[]{:S(2)}) collective-permute-start(bf16[64,4000]{1,0:T(8,128)(2,1)} %multiply_convert_fusion.15), channel_id=1, source_target_pairs={{0,8},{8,16},{16,24},{1,9},{9,17},{17,25},{2,10},{10,18},{18,26},{... | collective-permute-start | bytes 1536008 | tf_op jit(solution)/shard_map/ppermute | solution.py:86
  142.7 3.2 copy.81
  148.1 3.2 copy.86
  154.8 3.1 copy.85
  158.0 3.2 copy.84
  163.1 4.6 %collective-permute-start.1 = (bf16[64,4000]{1,0:T(8,128)(2,1)S(1)}, bf16[64,4000]{1,0:T(8,128)(2,1)S(1)}, u32[]{:S(2)}, u32[]{:S(2)}) collective-permute-start(bf16[64,4000]{1,0:T(8,128)(2,1)S(1)} %multiply_convert_fusion.14), channel_id=1, source_target_pairs={{0,8},{8,16},{16,24},{1,9},{9,17},{17,25},{2,10},{10,18},{18,26},{... | collective-permute-start | bytes 1536008 | tf_op jit(solution)/shard_map/ppermute | solution.py:86
  172.8 6.0 %collective-permute-done.1 = bf16[64,4000]{1,0:T(8,128)(2,1)S(1)} collective-permute-done((bf16[64,4000]{1,0:T(8,128)(2,1)S(1)}, bf16[64,4000]{1,0:T(8,128)(2,1)S(1)}, u32[]{:S(2)}, u32[]{:S(2)}) %collective-permute-start.1) | collective-permute-done | bytes 512032 | tf_op jit(solution)/shard_map/ppermute | solution.py:86
  180.0 5.2 %collective-permute-start.2 = (bf16[64,4000]{1,0:T(8,128)(2,1)}, bf16[64,4000]{1,0:T(8,128)(2,1)}, u32[]{:S(2)}, u32[]{:S(2)}) collective-permute-start(bf16[64,4000]{1,0:T(8,128)(2,1)} %multiply_convert_fusion.13), channel_id=1, source_target_pairs={{0,8},{8,16},{16,24},{1,9},{9,17},{17,25},{2,10},{10,18},{18,26},{... | collective-permute-start | bytes 1536008 | tf_op jit(solution)/shard_map/ppermute | solution.py:86
  191.1 3.2 copy.83
  194.9 7.1 %collective-permute-done.5 = bf16[64,4000]{1,0:T(8,128)(2,1)} collective-permute-done((bf16[64,4000]{1,0:T(8,128)(2,1)}, bf16[64,4000]{1,0:T(8,128)(2,1)}, u32[]{:S(2)}, u32[]{:S(2)}) %collective-permute-start.5) | collective-permute-done | bytes 512032 | tf_op jit(solution)/shard_map/ppermute | solution.py:87
  202.0 3.7 multiply_convert_fusion.8
  205.7 3.6 collective-permute-start.6
  210.5 16.0 %all_gather.30 = bf16[384,512]{1,0:T(8,128)(2,1)} all-gather(bf16[192,512]{1,0:T(8,128)(2,1)S(1)} %copy-done.2), channel_id=1, replica_groups={{0,8},{16,24},{1,9},{17,25},{2,10},{18,26},{3,11},{19,27},{4,12},{20,28..., dimensions={0}, use_global_device_ids=true | all-gather | bytes 589824 | tf_op jit(solution)/shard_map/all_gather | solution.py:57
  231.9 3.8 %multiply_convert_fusion.6 = (bf16[64,4000]{1,0:T(8,128)(2,1)}, f32[384,4000]{1,0:T(8,128)}, bf16[64,4000]{1,0:T(8,128)(2,1)}) fusion(bf16[64,4000]{1,0:T(8,128)(2,1)} %collective-permute-done.7, f32[64,4000]{1,0:T(8,128)} %copy.88, f32[64]{0:T(128)S(1)} %get-tuple-element.65, f32[384,4000]{1,0:T(8,128)} %get-tuple-element.43, ...), kind=kLoop, calls=%fused_computation.23 | loop fusion | flops 4352000 | bytes 5218817 | tf_op jit(solution)/shard_map/convert_element_type | solution.py:13
  245.0 4.9 %collective-permute-done.9 = bf16[64,4000]{1,0:T(8,128)(2,1)} collective-permute-done((bf16[64,4000]{1,0:T(8,128)(2,1)}, bf16[64,4000]{1,0:T(8,128)(2,1)}, u32[]{:S(2)}, u32[]{:S(2)}) %collective-permute-start.9) | collective-permute-done | bytes 512032 | tf_op jit(solution)/shard_map/ppermute | solution.py:87
  249.9 3.7 multiply_convert_fusion.4
  253.6 3.9 %collective-permute-start.10 = (bf16[64,4000]{1,0:T(8,128)(2,1)}, bf16[64,4000]{1,0:T(8,128)(2,1)}, u32[]{:S(2)}, u32[]{:S(2)}) collective-permute-start(bf16[64,4000]{1,0:T(8,128)(2,1)} %get-tuple-element.38), channel_id=1, source_target_pairs={{0,8},{8,16},{16,24},{1,9},{9,17},{17,25},{2,10},{10,18},{18,26},{... | collective-permute-start | bytes 1536008 | tf_op jit(solution)/shard_map/ppermute | solution.py:86
  264.2 4.6 %collective-permute-done.11 = bf16[64,4000]{1,0:T(8,128)(2,1)} collective-permute-done((bf16[64,4000]{1,0:T(8,128)(2,1)}, bf16[64,4000]{1,0:T(8,128)(2,1)}, u32[]{:S(2)}, u32[]{:S(2)}) %collective-permute-start.11) | collective-permute-done | bytes 512032 | tf_op jit(solution)/shard_map/ppermute | solution.py:87
  268.8 3.7 multiply_convert_fusion.2
  277.6 8.6 %all-reduce = s32[384]{0:T(512)S(1)} all-reduce(s32[384]{0:T(512)S(1)} %dynamic-update-slice), channel_id=1, replica_groups={{0,8},{16,24},{1,9},{17,25},{2,10},{18,26},{3,11},{19,27},{4,12},{20,28..., use_global_device_ids=true, to_apply=%add | all-reduce | flops 384 | bytes 3072
  291.5 3.8 %multiply_convert_fusion.1 = (bf16[64,4000]{1,0:T(8,128)(2,1)}, f32[384,4000]{1,0:T(8,128)}, bf16[64,4000]{1,0:T(8,128)(2,1)}) fusion(bf16[64,4000]{1,0:T(8,128)(2,1)} %collective-permute-done.12, f32[64,4000]{1,0:T(8,128)S(1)} %copy.93, f32[64]{0:T(128)S(1)} %get-tuple-element.60, f32[384,4000]{1,0:T(8,128)} %get-tuple-element.34, ...), kind=kLoop, calls=%fused_computation.10 | loop fusion | flops 4352000 | bytes 5218817 | tf_op jit(solution)/shard_map/convert_element_type | solution.py:13
  298.9 23.3 %select_reduce_fusion = (f32[384]{0:T(512)S(1)}, f32[384]{0:T(512)S(1)}, f32[384,4000]{0,1:T(8,128)}) fusion(s32[384]{0:T(512)S(1)} %all-reduce, s32[4000]{0:T(1024)S(1)} %iota_add_fusion, bf16[384,4096]{1,0:T(8,128)(2,1)} %all-gather.10.cloned.1.call-done, bf16[4096,4000]{0,1:T(8,128)(2,1)} %param.10), kind=kOutput, calls=%fused_computation.7 | convolution fusion | flops 12589056000 | bytes 42078336 | tf_op jit(solution)/shard_map/dot_general | solution.py:21
  322.1 6.6 %copy.53 = f32[384,4000]{1,0:T(8,128)} copy(f32[384,4000]{0,1:T(8,128)} %get-tuple-element.77) | data formatting | bytes 12288000 | tf_op jit(solution)/shard_map/dot_general | solution.py:21
  332.5 3.4 select_dynamic-update-slice_fusion
  335.9 6.3 %multiply_reduce_fusion = (f32[384]{0:T(512)S(1)}, f32[384]{0:T(512)S(1)}, f32[384]{0:T(512)S(1)}) fusion(f32[384,4000]{1,0:T(8,128)} %select_dynamic-update-slice_fusion, f32[384,4000]{1,0:T(8,128)} %copy.53, f32[384]{0:T(512)S(1)} %get-tuple-element.6), kind=kLoop, calls=%fused_computation.5 | loop fusion | flops 10750848 | bytes 12294144 | tf_op jit(solution)/shard_map/reduce_sum | solution.py:95
  342.3 8.2 %all-gather.5 = f32[8,5,384]{2,1,0:T(8,128)S(1)} all-gather(f32[1,5,384]{2,1,0:T(8,128)S(1)} %bitcast.54), channel_id=4, replica_groups=mesh['branch'=4,'vocab'=8] {'vocab'}, dimensions={0}, use_global_device_ids=true | all-gather | bytes 69120 | tf_op jit(solution)/shard_map/all_gather | solution.py:97
  350.7 13.0 %all-gather.6 = f32[4,2,384]{2,1,0:T(2,128)S(1)} all-gather(f32[1,2,384]{2,1,0:T(2,128)S(1)} %maximum_bitcast_fusion.1), channel_id=5, replica_groups=mesh['branch'=4,'vocab'=8] {'branch'}, dimensions={0}, use_global_device_ids=true | all-gather | bytes 15360 | tf_op jit(solution)/shard_map/all_gather | solution.py:103
  (91 shorter events, 72.2 us)
Async XLA Ops:
  7.2 52.1 %all-gather.12.cloned.1.call-start = ((), (), s32[]{:S(2)}) async-start(), calls=%async_computation.1 | async-start | bytes 7077888 | tf_op jit(solution)/shard_map/all_gather | solution.py:55
  7.9 291.0 %all-gather.10.cloned.1.call-start = ((), (), s32[]{:S(2)}) async-start(), calls=%async_computation | async-start | bytes 3538944 | tf_op jit(solution)/shard_map/all_gather | solution.py:59
  90.7 4.5 %copy-start = (f32[768,4000]{0,1:T(8,128)}, f32[768,4000]{0,1:T(8,128)S(1)}, u32[]{:S(2)}) copy-start(f32[768,4000]{0,1:T(8,128)S(1)} %get-tuple-element.79) | copy-start | bytes 36864004
  139.0 22.2 %collective-permute-start = (bf16[64,4000]{1,0:T(8,128)(2,1)}, bf16[64,4000]{1,0:T(8,128)(2,1)}, u32[]{:S(2)}, u32[]{:S(2)}) collective-permute-start(bf16[64,4000]{1,0:T(8,128)(2,1)} %multiply_convert_fusion.15), channel_id=1, source_target_pairs={{0,8},{8,16},{16,24},{1,9},{9,17},{17,25},{2,10},{10,18},{18,26},{... | collective-permute-start | bytes 1536008 | tf_op jit(solution)/shard_map/ppermute | solution.py:86
  153.6 16.1 %collective-permute-start.3 = (bf16[64,4000]{1,0:T(8,128)(2,1)}, bf16[64,4000]{1,0:T(8,128)(2,1)}, u32[]{:S(2)}, u32[]{:S(2)}) collective-permute-start(bf16[64,4000]{1,0:T(8,128)(2,1)} %multiply_convert_fusion.12), channel_id=1, source_target_pairs={{8,0},{16,8},{24,16},{9,1},{17,9},{25,17},{10,2},{18,10},{26,18},{... | collective-permute-start | bytes 1536008 | tf_op jit(solution)/shard_map/ppermute | solution.py:87
  161.2 25.2 %copy-start.1 = (f32[64,4000]{1,0:T(8,128)S(1)}, f32[64,4000]{1,0:T(8,128)}, u32[]{:S(2)}) copy-start(f32[64,4000]{1,0:T(8,128)} %copy.84) | copy-start | bytes 3072004
  163.1 15.7 %collective-permute-start.1 = (bf16[64,4000]{1,0:T(8,128)(2,1)S(1)}, bf16[64,4000]{1,0:T(8,128)(2,1)S(1)}, u32[]{:S(2)}, u32[]{:S(2)}) collective-permute-start(bf16[64,4000]{1,0:T(8,128)(2,1)S(1)} %multiply_convert_fusion.14), channel_id=1, source_target_pairs={{0,8},{8,16},{16,24},{1,9},{9,17},{17,25},{2,10},{10,18},{18,26},{... | collective-permute-start | bytes 1536008 | tf_op jit(solution)/shard_map/ppermute | solution.py:86
  171.5 14.9 %collective-permute-start.4 = (bf16[64,4000]{1,0:T(8,128)(2,1)S(1)}, bf16[64,4000]{1,0:T(8,128)(2,1)S(1)}, u32[]{:S(2)}, u32[]{:S(2)}) collective-permute-start(bf16[64,4000]{1,0:T(8,128)(2,1)S(1)} %multiply_convert_fusion.11), channel_id=1, source_target_pairs={{8,0},{16,8},{24,16},{9,1},{17,9},{25,17},{10,2},{18,10},{26,18},{... | collective-permute-start | bytes 1536008 | tf_op jit(solution)/shard_map/ppermute | solution.py:87
  180.0 14.9 %collective-permute-start.2 = (bf16[64,4000]{1,0:T(8,128)(2,1)}, bf16[64,4000]{1,0:T(8,128)(2,1)}, u32[]{:S(2)}, u32[]{:S(2)}) collective-permute-start(bf16[64,4000]{1,0:T(8,128)(2,1)} %multiply_convert_fusion.13), channel_id=1, source_target_pairs={{0,8},{8,16},{16,24},{1,9},{9,17},{17,25},{2,10},{10,18},{18,26},{... | collective-permute-start | bytes 1536008 | tf_op jit(solution)/shard_map/ppermute | solution.py:86
  186.4 24.1 %copy-start.2 = (bf16[192,512]{1,0:T(8,128)(2,1)S(1)}, bf16[192,512]{1,0:T(8,128)(2,1)}, u32[]{:S(2)}) copy-start(bf16[192,512]{1,0:T(8,128)(2,1)} %param.9) | copy-start | bytes 589828
  187.7 14.3 %collective-permute-start.5 = (bf16[64,4000]{1,0:T(8,128)(2,1)}, bf16[64,4000]{1,0:T(8,128)(2,1)}, u32[]{:S(2)}, u32[]{:S(2)}) collective-permute-start(bf16[64,4000]{1,0:T(8,128)(2,1)} %multiply_convert_fusion.10), channel_id=1, source_target_pairs={{8,0},{16,8},{24,16},{9,1},{17,9},{25,17},{10,2},{18,10},{26,18},{... | collective-permute-start | bytes 1536008 | tf_op jit(solution)/shard_map/ppermute | solution.py:87
  205.7 26.2 %collective-permute-start.6 = (bf16[64,4000]{1,0:T(8,128)(2,1)}, bf16[64,4000]{1,0:T(8,128)(2,1)}, u32[]{:S(2)}, u32[]{:S(2)}) collective-permute-start(bf16[64,4000]{1,0:T(8,128)(2,1)} %get-tuple-element.44), channel_id=1, source_target_pairs={{0,8},{8,16},{16,24},{1,9},{9,17},{17,25},{2,10},{10,18},{18,26},{... | collective-permute-start | bytes 1536008 | tf_op jit(solution)/shard_map/ppermute | solution.py:86
  209.2 22.7 %collective-permute-start.7 = (bf16[64,4000]{1,0:T(8,128)(2,1)}, bf16[64,4000]{1,0:T(8,128)(2,1)}, u32[]{:S(2)}, u32[]{:S(2)}) collective-permute-start(bf16[64,4000]{1,0:T(8,128)(2,1)} %get-tuple-element.42), channel_id=1, source_target_pairs={{8,0},{16,8},{24,16},{9,1},{17,9},{25,17},{10,2},{18,10},{26,18},{... | collective-permute-start | bytes 1536008 | tf_op jit(solution)/shard_map/ppermute | solution.py:87
  235.7 9.3 %collective-permute-start.8 = (bf16[64,4000]{1,0:T(8,128)(2,1)}, bf16[64,4000]{1,0:T(8,128)(2,1)}, u32[]{:S(2)}, u32[]{:S(2)}) collective-permute-start(bf16[64,4000]{1,0:T(8,128)(2,1)} %get-tuple-element.41), channel_id=1, source_target_pairs={{0,8},{8,16},{16,24},{1,9},{9,17},{17,25},{2,10},{10,18},{18,26},{... | collective-permute-start | bytes 1536008 | tf_op jit(solution)/shard_map/ppermute | solution.py:86
  237.8 12.0 %collective-permute-start.9 = (bf16[64,4000]{1,0:T(8,128)(2,1)}, bf16[64,4000]{1,0:T(8,128)(2,1)}, u32[]{:S(2)}, u32[]{:S(2)}) collective-permute-start(bf16[64,4000]{1,0:T(8,128)(2,1)} %get-tuple-element.39), channel_id=1, source_target_pairs={{8,0},{16,8},{24,16},{9,1},{17,9},{25,17},{10,2},{18,10},{26,18},{... | collective-permute-start | bytes 1536008 | tf_op jit(solution)/shard_map/ppermute | solution.py:87
  253.6 22.6 %copy-start.4 = (u32[32]{0:T(128)S(1)}, u32[32]{0:T(128)}, u32[]{:S(2)}) copy-start(u32[32]{0:T(128)} %constant.77) | copy-start | bytes 388
  253.6 23.8 %copy-start.3 = (s32[192]{0:T(256)S(1)}, s32[192]{0:T(256)}, u32[]{:S(2)}) copy-start(s32[192]{0:T(256)} %param.13) | copy-start | bytes 2308
  253.6 10.7 %collective-permute-start.10 = (bf16[64,4000]{1,0:T(8,128)(2,1)}, bf16[64,4000]{1,0:T(8,128)(2,1)}, u32[]{:S(2)}, u32[]{:S(2)}) collective-permute-start(bf16[64,4000]{1,0:T(8,128)(2,1)} %get-tuple-element.38), channel_id=1, source_target_pairs={{0,8},{8,16},{16,24},{1,9},{9,17},{17,25},{2,10},{10,18},{18,26},{... | collective-permute-start | bytes 1536008 | tf_op jit(solution)/shard_map/ppermute | solution.py:86
  257.4 11.4 %collective-permute-start.11 = (bf16[64,4000]{1,0:T(8,128)(2,1)}, bf16[64,4000]{1,0:T(8,128)(2,1)}, u32[]{:S(2)}, u32[]{:S(2)}) collective-permute-start(bf16[64,4000]{1,0:T(8,128)(2,1)} %get-tuple-element.36), channel_id=1, source_target_pairs={{8,0},{16,8},{24,16},{9,1},{17,9},{25,17},{10,2},{18,10},{26,18},{... | collective-permute-start | bytes 1536008 | tf_op jit(solution)/shard_map/ppermute | solution.py:87
  272.5 19.0 %collective-permute-start.12 = (bf16[64,4000]{1,0:T(8,128)(2,1)}, bf16[64,4000]{1,0:T(8,128)(2,1)}, u32[]{:S(2)}, u32[]{:S(2)}) collective-permute-start(bf16[64,4000]{1,0:T(8,128)(2,1)} %get-tuple-element.35), channel_id=1, source_target_pairs={{0,8},{8,16},{16,24},{1,9},{9,17},{17,25},{2,10},{10,18},{18,26},{... | collective-permute-start | bytes 1536008 | tf_op jit(solution)/shard_map/ppermute | solution.py:86
  274.8 16.7 %collective-permute-start.13 = (bf16[64,4000]{1,0:T(8,128)(2,1)}, bf16[64,4000]{1,0:T(8,128)(2,1)}, u32[]{:S(2)}, u32[]{:S(2)}) collective-permute-start(bf16[64,4000]{1,0:T(8,128)(2,1)} %get-tuple-element.33), channel_id=1, source_target_pairs={{8,0},{16,8},{24,16},{9,1},{17,9},{25,17},{10,2},{18,10},{26,18},{... | collective-permute-start | bytes 1536008 | tf_op jit(solution)/shard_map/ppermute | solution.py:87
  295.3 37.3 %collective-permute-start.14 = (bf16[64,4000]{1,0:T(8,128)(2,1)}, bf16[64,4000]{1,0:T(8,128)(2,1)}, u32[]{:S(2)}, u32[]{:S(2)}) collective-permute-start(bf16[64,4000]{1,0:T(8,128)(2,1)} %get-tuple-element.30), channel_id=1, source_target_pairs={{0,8},{8,16},{16,24},{1,9},{9,17},{17,25},{2,10},{10,18},{18,26},{... | collective-permute-start | bytes 1536008 | tf_op jit(solution)/shard_map/ppermute | solution.py:86
  297.6 35.0 %collective-permute-start.15 = (bf16[64,4000]{1,0:T(8,128)(2,1)}, bf16[64,4000]{1,0:T(8,128)(2,1)}, u32[]{:S(2)}, u32[]{:S(2)}) collective-permute-start(bf16[64,4000]{1,0:T(8,128)(2,1)} %get-tuple-element.32), channel_id=1, source_target_pairs={{8,0},{16,8},{24,16},{9,1},{17,9},{25,17},{10,2},{18,10},{26,18},{... | collective-permute-start | bytes 1536008 | tf_op jit(solution)/shard_map/ppermute | solution.py:87
Sparse Core Ops, SparseCore 0:
  9.9 49.3 all-gather.11
  226.7 30.0 all-gather.9

commit v2 on v0

v2 whole, which is shorter than its diff:
```python
import functools

import jax
import jax.numpy as jnp
from jax import lax
from jax.experimental import pallas as pl
from jax.experimental.pallas import tpu as pltpu
from jax.sharding import PartitionSpec as P

MESH = pl.DeviceIdType.MESH
SCALE = 2.0**30
LOG_SCALE = 20.79441541679836
PIECES = 32
BLOCK = 80
TILE = 800
SLOTS = 3
LAG = 2


def divisor(width, most):
    return max(t for t in range(8, most + 1, 8) if width % t == 0)


def piece_rows(width):
    return min(t for t in range(8, width + 1, 8) if width % t == 0 and width // t <= PIECES)


def flip(chip, e, chips):
    out, bit = 0, 1
    while bit < chips:
        out = out + bit * ((chip // bit + e // bit) % 2)
        bit *= 2
    return out


def kernel(
    n, nv, hidden, weight, student, s_weight, branch_weight, assignment, targets, out,
    hid, shid, wbuf, acc, sacc, up_in, down_in, up_out, down_out, factor, rows_in, fin_in, tbuf, res,
    local_sem, w_sem, h_send, h_recv, s_send, s_recv, p_send, p_recv, t_send, t_recv,
    up_send, up_recv, down_send, down_recv, l_send, l_recv, f_send, f_recv, r_send, r_recv,
):
    z, v = lax.axis_index("branch"), lax.axis_index("vocab")
    chips = nv // 2
    chip, core = v // 2, v % 2
    sibling = v + 1 - 2 * core
    half_n = n // 2
    tokens, feat = hid.shape[1], hid.shape[2]
    half, per, width = tokens // 2, tokens // n, acc.shape[0]
    rows_each = piece_rows(width)
    pieces = width // rows_each
    block, tile_rows = divisor(width, BLOCK), divisor(width, TILE)
    upper = z // half_n
    end = upper * (n - 1)
    is_end = z == end
    place = z % half_n

    def remote(src, dst, send, recv, zz, vv):
        return pltpu.make_async_remote_copy(
            src_ref=src, dst_ref=dst, send_sem=send, recv_sem=recv, device_id=(zz, vv), device_id_type=MESH
        )

    def owner(s):
        return flip(chip, s // 2, chips) * 2 + (core + s) % 2

    def fetch(src, s):
        slot = s % SLOTS
        features = pl.ds(pl.multiple_of(owner(s) * feat, feat), feat)
        return pltpu.make_async_copy(src.at[:, features], wbuf.at[slot], w_sem.at[slot])

    t_weight = weight.at[0]
    own = pltpu.make_async_copy(hidden.at[0], hid.at[0], local_sem.at[0])
    own.start()
    mine = pl.ds(pl.multiple_of(place * per, per), per)
    own_student = pltpu.make_async_copy(student, shid.at[0, mine], local_sem.at[1])
    own_targets = pltpu.make_async_copy(targets, tbuf.at[place], local_sem.at[2])

    @pl.when(is_end)
    def _():
        own_student.start()
        own_targets.start()

    fetch(t_weight, 0).start()
    fetch(t_weight, 1).start()

    barrier = pltpu.get_barrier_semaphore()
    for d in range(1, nv):
        pl.semaphore_signal(barrier, inc=1, device_id=(z, (v + d) % nv), device_id_type=MESH)
    for d in range(1, n):
        pl.semaphore_signal(barrier, inc=1, device_id=((z + d) % n, v), device_id_type=MESH)
    own.wait()
    pl.semaphore_wait(barrier, nv - 1 + n - 1)

    def push(buf, send, recv, e):
        return remote(buf.at[0], buf.at[2 * e], send.at[2 * e], recv.at[2 * e], z, flip(chip, e, chips) * 2 + core)

    def forward(buf, send, recv, e):
        return remote(buf.at[2 * e], buf.at[2 * e + 1], send.at[2 * e + 1], recv.at[2 * e + 1], z, sibling)

    def begin(buf, send, recv):
        forward(buf, send, recv, 0).start()
        for e in range(1, min(3, chips)):
            push(buf, send, recv, e).start()

    def chunk_step(s, buf, send, recv, src, total):
        @pl.when(s + 2 < nv)
        def _():
            fetch(src, s + 2).start()

        e = s // 2

        @pl.when((s % 2 == 0) & (s > 0))
        def _():
            push(buf, send, recv, e).wait_recv()
            forward(buf, send, recv, e).start()

            @pl.when(e + 2 < chips)
            def _():
                push(buf, send, recv, e + 2).start()

        @pl.when(s % 2 == 1)
        def _():
            forward(buf, send, recv, e).wait_recv()

        fetch(src, s).wait()
        slot = s % SLOTS

        @pl.loop(0, width // tile_rows)
        def _(j):
            rows = pl.ds(pl.multiple_of(j * tile_rows, tile_rows), tile_rows)
            total[rows, :] += lax.dot_general(
                wbuf[slot, rows, :], buf[s], (((1,), (1,)), ((), ())), preferred_element_type=jnp.float32
            )

    def finish_sends(buf, send, recv):
        @pl.loop(0, chips)
        def _(e):
            forward(buf, send, recv, e).wait_send()

        @pl.loop(1, chips)
        def _(e):
            push(buf, send, recv, e).wait_send()

    begin(hid, h_send, h_recv)

    pass_student = remote(student, shid.at[0, mine], p_send, p_recv.at[place], end, v)
    pass_targets = remote(targets, tbuf.at[place], t_send, t_recv.at[place], end, v)

    @pl.when(z != end)
    def _():
        pass_student.start()
        pass_targets.start()

    def block_rows(i):
        return pl.ds(pl.multiple_of(i * block, block), block)

    @pl.loop(0, width // block)
    def _(i):
        acc[block_rows(i), :] = jnp.zeros((block, tokens), jnp.float32)

    @pl.loop(0, nv)
    def _(s):
        chunk_step(s, hid, h_send, h_recv, t_weight, acc)

    @pl.when(is_end)
    def _():
        fetch(s_weight, 0).start()
        fetch(s_weight, 1).start()
        own_student.wait()
        own_targets.wait()

        @pl.loop(0, half_n)
        def _(j):
            @pl.when(j != place)
            def _():
                there = pl.ds(pl.multiple_of(j * per, per), per)
                remote(student, shid.at[0, there], p_send, p_recv.at[j], z, v).wait_recv()
                remote(targets, tbuf.at[j], t_send, t_recv.at[j], z, v).wait_recv()

        begin(shid, s_send, s_recv)

        @pl.loop(0, width // block)
        def _(i):
            sacc[block_rows(i), :] = jnp.zeros((block, half), jnp.float32)

    def fold(x, reduce):
        return reduce(x.reshape(block // 8, 8, x.shape[1]), axis=0)

    def highest(logits):
        low = jnp.full((8, logits.shape[1]), -jnp.inf, jnp.float32)
        top = lax.fori_loop(
            0, width // block, lambda i, top: jnp.maximum(top, fold(logits[block_rows(i), :], jnp.max)), low
        )
        return jnp.max(top, axis=0, keepdims=True)

    def rows_of(*values):
        row = lax.broadcasted_iota(jnp.int32, (8, values[0].shape[1]), 0)
        packed = jnp.zeros(row.shape, jnp.float32)
        for i, value in enumerate(values):
            packed = jnp.where(row == i, value, packed)
        return packed

    top = highest(acc)

    def exponentials(i, total):
        x = jnp.exp(acc[block_rows(i), :] - top)
        acc[block_rows(i), :] = x
        return total + fold(x, jnp.sum)

    total = lax.fori_loop(0, width // block, exponentials, jnp.zeros((8, tokens), jnp.float32))
    rows_in[0] = rows_of(top, jnp.sum(total, axis=0, keepdims=True))

    def exchange(buf, send, recv):
        @pl.loop(1, nv)
        def _(d):
            remote(buf.at[0], buf.at[d], send.at[d], recv.at[d], z, (v + d) % nv).start()

        @pl.loop(1, nv)
        def _(d):
            remote(buf.at[0], buf.at[d], send.at[d], recv.at[d], z, (v + d) % nv).wait()

    def merge(buf):
        top = buf[0, 0:1, :]
        for d in range(1, nv):
            top = jnp.maximum(top, buf[d, 0:1, :])
        total = jnp.zeros_like(top)
        for d in range(nv):
            total += buf[d, 1:2, :] * jnp.exp(buf[d, 0:1, :] - top)
        return top + jnp.log(total)

    exchange(rows_in, l_send, l_recv)
    weights = branch_weight[...]
    log_share = jnp.log(weights / jnp.sum(weights, axis=1, keepdims=True))
    index = lax.broadcasted_iota(jnp.int32, weights.shape, 1)
    chosen = jnp.sum(
        jnp.where(index == z, assignment[...].astype(jnp.float32), 0.0), axis=1, keepdims=True
    )
    own_share = jnp.sum(
        jnp.where(index.astype(jnp.float32) == chosen, log_share, 0.0), axis=1, keepdims=True
    )
    scale = jnp.exp(rows_in[0, 0:1, :] - merge(rows_in) + own_share) * SCALE
    factor[...] = jnp.broadcast_to(scale, (8, tokens))

    def piece_up(c):
        return remote(up_out.at[c], up_in.at[c], up_send.at[c], up_recv.at[c], lax.rem(z + 1, n), v)

    def piece_down(c):
        return remote(down_out.at[c], down_in.at[c], down_send.at[c], down_recv.at[c], lax.rem(z + n - 1, n), v)

    def turn(c, base, order, piece, came, leaves):
        rows = pl.ds(pl.multiple_of(c * rows_each, rows_each), rows_each)
        lanes = pl.ds(base, half)

        @pl.when(order == 0)
        def _():
            p = acc[rows, lanes] * factor[:1, lanes]
            p = p * p
            leaves[c] = (p * p).astype(jnp.bfloat16)
            piece(c).start()

        @pl.when(order > 0)
        def _():
            piece(c).wait_recv()
            p = acc[rows, lanes] * factor[:1, lanes] + lax.rsqrt(lax.rsqrt(came[c].astype(jnp.float32)))

            @pl.when(order < n - 1)
            def _():
                square = p * p
                leaves[c] = (square * square).astype(jnp.bfloat16)
                piece(c).start()

            @pl.when(order == n - 1)
            def _():
                acc[rows, lanes] = p

    first_student = LAG * (n - 1) - 2

    @pl.loop(0, max(pieces + LAG * (n - 1), first_student + nv))
    def _(k):
        c = k - LAG * z

        @pl.when((c >= 0) & (c < pieces))
        def _():
            turn(c, half, z, piece_up, up_in, up_out)

        o = n - 1 - z
        d = k - LAG * o

        @pl.when((d >= 0) & (d < pieces))
        def _():
            turn(d, 0, o, piece_down, down_in, down_out)

        s = k - first_student

        @pl.when(is_end & (s >= 0) & (s < nv))
        def _():
            chunk_step(s, shid, s_send, s_recv, s_weight, sacc)

    @pl.when(is_end)
    def _():
        lanes = pl.ds(pl.multiple_of(upper * half, half), half)
        s_top = highest(sacc)
        picks = tbuf[0]
        for j in range(1, half_n):
            picks = picks + tbuf[j]
        picks = picks[:1] - v * width
        vocab_row = lax.broadcasted_iota(jnp.int32, (block, half), 0)

        def terms(i, sums):
            x = sacc[block_rows(i), :]
            q = acc[block_rows(i), lanes]
            hit = jnp.where(vocab_row + i * block == picks, x, 0.0)
            x = x - s_top
            mixture = jnp.log(jnp.maximum(q, 1e-30)) - LOG_SCALE
            q = q * (1.0 / SCALE)
            new = (jnp.exp(x), hit, q * (mixture - x), q)
            return tuple(old + fold(value, jnp.sum) for old, value in zip(sums, new))

        sums = lax.fori_loop(0, width // block, terms, (jnp.zeros((8, half), jnp.float32),) * 4)
        fin_in[0] = rows_of(s_top, *(jnp.sum(value, axis=0, keepdims=True) for value in sums))
        exchange(fin_in, f_send, f_recv)
        lse = merge(fin_in)
        hit, cross, mass = (jnp.zeros((1, half), jnp.float32) for _ in range(3))
        for d in range(nv):
            hit += fin_in[d, 2:3, :]
            mass += fin_in[d, 4:5, :]
            cross += fin_in[d, 3:4, :] + fin_in[d, 4:5, :] * (lse - fin_in[d, 0:1, :])
        row = lax.broadcasted_iota(jnp.int32, (8, half), 0)
        res[...] = jnp.where(row == 0, cross / mass - jnp.log(mass), lse - hit)

        def give(j):
            return remote(res, res, r_send.at[j], r_recv, upper * half_n + j, v)

        for act in ("start", "wait_send"):
            @pl.loop(0, half_n)
            def _(j):
                @pl.when(j != place)
                def _():
                    getattr(give(j), act)()

        finish_sends(shid, s_send, s_recv)

    @pl.when(z != end)
    def _():
        remote(res, res, r_send.at[0], r_recv, end, v).wait_recv()
        pass_student.wait_send()
        pass_targets.wait_send()

    out[...] = res[...]
    finish_sends(hid, h_send, h_recv)

    @pl.loop(0, pieces)
    def _(c):
        @pl.when(z < n - 1)
        def _():
            piece_up(c).wait_send()

        @pl.when(z > 0)
        def _():
            piece_down(c).wait_send()


def per_device(
    teacher_hidden,
    teacher_weight,
    student_hidden,
    student_weight,
    branch_weight,
    assignment,
    targets,
):
    n, nv = lax.axis_size("branch"), lax.axis_size("vocab")
    _, tokens, feat = teacher_hidden.shape
    width = teacher_weight.shape[2]
    half, per = tokens // 2, tokens // n
    rows_each = piece_rows(width)
    pieces = width // rows_each
    first = lax.axis_index("branch") % (n // 2) * per
    spread = jnp.zeros((8, half), jnp.int32)
    spread = lax.dynamic_update_slice(spread, jnp.broadcast_to(targets[None], (8, per)), (0, first))
    f32, bf16 = jnp.float32, jnp.bfloat16
    dma = pltpu.SemaphoreType.DMA
    anywhere = pl.BlockSpec(memory_space=pl.ANY)
    vmem = pl.BlockSpec(memory_space=pltpu.VMEM)
    result = pl.pallas_call(
        functools.partial(kernel, n, nv),
        out_shape=jax.ShapeDtypeStruct((8, half), f32),
        in_specs=[anywhere, anywhere, anywhere, anywhere, vmem, vmem, vmem],
        out_specs=vmem,
        scratch_shapes=[
            pltpu.VMEM((nv, tokens, feat), bf16),
            pltpu.VMEM((nv, half, feat), bf16),
            pltpu.VMEM((SLOTS, width, feat), bf16),
            pltpu.VMEM((width, tokens), f32),
            pltpu.VMEM((width, half), f32),
            pltpu.VMEM((pieces, rows_each, half), bf16),
            pltpu.VMEM((pieces, rows_each, half), bf16),
            pltpu.VMEM((pieces, rows_each, half), bf16),
            pltpu.VMEM((pieces, rows_each, half), bf16),
            pltpu.VMEM((8, tokens), f32),
            pltpu.VMEM((nv, 8, tokens), f32),
            pltpu.VMEM((nv, 8, half), f32),
            pltpu.VMEM((n // 2, 8, half), jnp.int32),
            pltpu.VMEM((8, half), f32),
            dma((3,)),
            dma((SLOTS,)),
            dma((nv,)), dma((nv,)),
            dma((nv,)), dma((nv,)),
            dma, dma((n // 2,)),
            dma, dma((n // 2,)),
            dma((pieces,)), dma((pieces,)),
            dma((pieces,)), dma((pieces,)),
            dma((nv,)), dma((nv,)),
            dma((nv,)), dma((nv,)),
            dma((n // 2,)), dma,
        ],
        compiler_params=pltpu.CompilerParams(
            collective_id=0, has_side_effects=True, vmem_limit_bytes=60 * 2**20
        ),
    )(
        teacher_hidden,
        jnp.swapaxes(teacher_weight, 1, 2),
        student_hidden,
        student_weight.T,
        branch_weight[None],
        assignment[None],
        spread,
    )
    mine = lax.dynamic_slice(result, (0, first), (2, per))
    return mine[0], mine[1]


def solution(mesh):
    in_specs = (
        P("branch", None, "vocab"),
        P("branch", None, "vocab"),
        P("branch", "vocab"),
        P(None, "vocab"),
        P(),
        P(),
        P("branch"),
    )
    out_specs = (P("branch"), P("branch"))
    return jax.shard_map(
        per_device, mesh=mesh, in_specs=in_specs, out_specs=out_specs, check_vma=False
    )
```

time: 532 us -> 159 us (0.30)
  waiting for transfers between devices: 331 us -> 0 us
  Pallas kernels: 0 us -> 155 us
  matrix products: 49.5 us -> 0 us
  local copies, waits for them, and re-layouts: 50.6 us -> 2.87 us
  other arithmetic: 41 us -> 0 us
  blocking collectives: 37.7 us -> 0 us
  between operations: 14.1 us -> 0.67 us
  starting transfers between devices: 6.59 us -> 0 us
    all_to_all x1 -> x0, waiting for transfers between devices: 273 us -> none  [per_device(): lax.all_to_all(shifted[None], 'branch', split_axis=1, concat_axis=0, tile...]
    pallas_call x0 -> x1, Pallas kernels: none -> 155 us  [per_device(): pl.pallas_call(functools.partial(kernel, n, nv), out_shape=jax.ShapeDtype...]
    all_gather x2 -> x0, waiting for transfers between devices: 56.9 us -> none  [the longest x1 31.6 us: per_device(): lax.all_gather(hidden_rows, 'vocab', axis=1, tiled=True)]
    dot_general x2 -> x0, matrix products: 49.5 us -> none  [add_product(): return jnp.dot(piece, weights, preferred_element_type=jnp.float32)]
    broadcast_in_dim x1 -> x2, local copies, waits for them, and re-layouts: 28.3 us -> 0.68 us  [the longest x1 0.68 us: per_device(): jnp.broadcast_to(targets[None], (8, per))]
    psum x2 -> x0, blocking collectives: 24.4 us -> none  [the longest x1 12.4 us: per_device(): divergence, target_loss = lax.psum((kl_terms, target_terms), 'vocab')]
    reduce_sum x6 -> x0, other arithmetic: 22.3 us -> none  [the longest x1 9.36 us: per_device(): jnp.sum(jnp.exp(gathered - highest[None]), axis=0)]
    unnamed x5 -> x2, local copies, waits for them, and re-layouts: 21.7 us -> 0.59 us
  transfers between devices with their start and end apart: 3 -> 0, of which waited for: 3 -> 0; matrix products, arithmetic and copies ran while one was open for 4% -> 0% of each run, Pallas kernels for 0% -> 0%
where the time goes in v2:
time: 159 us
  Pallas kernels  155 us (97%)
  local copies, waits for them, and re-layouts  2.87 us (2%)
    pallas_call x1, Pallas kernels, per_device(): pl.pallas_call(functools.partial(kernel, n, nv), out_shape=jax.ShapeDtype...  155 us

profile of v2, /device:TPU:0, one launch (start us, length us, event | category | flops | bytes accessed | tf_op | source)
XLA Modules:
  0.0 158.6 jit_solution(1756755385218298407)
XLA Ops:
  0.6 0.7 broadcast_in_dim.18
  1.3 0.2 dynamic_update_slice.3.targets
  1.5 0.0 copy-start
  1.5 0.6 copy-done
  2.1 155.0 %shard_map.86 = f32[8,384]{1,0:T(8,128)} custom-call(bf16[1,768,512]{2,1,0:T(8,128)(2,1)} %hidden.1, bf16[1,4000,4096]{2,1,0:T(8,128)(2,1)} %bitcast.6, bf16[192,512]{1,0:T(8,128)(2,1)} %student.1, bf16[4000,4096]{1,0:T(8,128)(2,1)} %bitcast.7, f32[1,4]{1,0:T(1,128)} %bitcast.10, s32[1,4]{1,0:T(1,128)} %bitcast.11, s32[8,384]{1,0:T(8,128)} %copy-done), custom_call_target="tpu_custom_call" | custom-call | tf_op jit(solution)/shard_map/pallas_call | solution.py:384
  157.1 1.4 fusion
  (1 shorter events, 0.0 us)
Async XLA Ops:
  1.5 0.6 copy-start

commit v3 on v2

v3 whole, which is shorter than its diff:
```python
import functools

import jax
import jax.numpy as jnp
from jax import lax
from jax.experimental import pallas as pl
from jax.experimental.pallas import tpu as pltpu
from jax.sharding import PartitionSpec as P

MESH = pl.DeviceIdType.MESH
SCALE = 2.0**30
LOG_SCALE = 20.79441541679836
LANES = 128
PIECES = 10
BLOCK = 80
TILE = 800
SLOTS = 4
LAG = 2


def divisor(width, most):
    return max(t for t in range(8, most + 1, 8) if width % t == 0)


def piece_rows(width):
    return min(t for t in range(8, width + 1, 8) if width % t == 0 and width // t <= PIECES)


def flip(chip, e, chips):
    out, bit = 0, 1
    while bit < chips:
        out = out + bit * ((chip // bit + e // bit) % 2)
        bit *= 2
    return out


def kernel(
    n, nv, hidden, weight, student, s_weight, branch_weight, assignment, targets, out,
    hid, shid, wbuf, acc, sacc, up_in, down_in, up_out, down_out, factor, s_top, rows_in, fin_in, tbuf, res,
    local_sem, w_sem, h_send, h_recv, s_send, s_recv, p_send, p_recv, t_send, t_recv,
    up_send, up_recv, down_send, down_recv, l_send, l_recv, f_send, f_recv, r_send, r_recv,
):
    z, v = lax.axis_index("branch"), lax.axis_index("vocab")
    chips = nv // 2
    chip, core = v // 2, v % 2
    sibling = v + 1 - 2 * core
    half_n = n // 2
    batches, feat = hid.shape[0], hid.shape[3]
    tokens = batches * 2 * LANES
    half, per, width = tokens // 2, tokens // n, acc.shape[1]
    rows_each = piece_rows(width)
    pieces = width // rows_each
    block, tile_rows = divisor(width, BLOCK), divisor(width, TILE)
    upper = z // half_n
    end = upper * (n - 1)
    is_end = z == end
    place = z % half_n

    def remote(src, dst, send, recv, zz, vv):
        return pltpu.make_async_remote_copy(
            src_ref=src, dst_ref=dst, send_sem=send, recv_sem=recv, device_id=(zz, vv), device_id_type=MESH
        )

    def owner(s):
        return flip(chip, s // 2, chips) * 2 + (core + s) % 2

    def fetch(src, q):
        s, slot = q % nv, q % SLOTS
        features = pl.ds(pl.multiple_of(owner(s) * feat, feat), feat)
        return pltpu.make_async_copy(src.at[:, features], wbuf.at[slot], w_sem.at[slot])

    def prefetch(q):
        @pl.when(q < batches * nv)
        def _():
            fetch(t_weight, q).start()

        @pl.when(is_end & (q >= batches * nv) & (q < (batches + 1) * nv))
        def _():
            fetch(s_weight, q).start()

    t_weight = weight.at[0]
    own = []
    for b in range(batches):
        for side in range(2):
            own.append(pltpu.make_async_copy(
                hidden.at[0, pl.ds(side * half + b * LANES, LANES)],
                hid.at[b, 0, pl.ds(side * LANES, LANES)],
                local_sem.at[2 + 2 * b + side],
            ))
            own[-1].start()
    mine = pl.ds(pl.multiple_of(place * per, per), per)
    own_student = pltpu.make_async_copy(student, shid.at[0, mine], local_sem.at[0])
    own_targets = pltpu.make_async_copy(targets, tbuf.at[place], local_sem.at[1])

    @pl.when(is_end)
    def _():
        own_student.start()
        own_targets.start()

    for q in range(SLOTS - 1):
        fetch(t_weight, q).start()

    def block_rows(i):
        return pl.ds(pl.multiple_of(i * block, block), block)

    def clear(b):
        @pl.loop(0, width // block)
        def _(i):
            acc[b, block_rows(i), :] = jnp.zeros((block, 2 * LANES), jnp.float32)

    barrier = pltpu.get_barrier_semaphore()
    for d in range(1, nv):
        pl.semaphore_signal(barrier, inc=1, device_id=(z, (v + d) % nv), device_id_type=MESH)
    for d in range(1, n):
        pl.semaphore_signal(barrier, inc=1, device_id=((z + d) % n, v), device_id_type=MESH)
    clear(0)
    for copy in own:
        copy.wait()
    pl.semaphore_wait(barrier, nv - 1 + n - 1)

    def push(buf, send, recv, e):
        return remote(buf.at[0], buf.at[2 * e], send.at[2 * e], recv.at[2 * e], z, flip(chip, e, chips) * 2 + core)

    def forward(buf, send, recv, e):
        return remote(buf.at[2 * e], buf.at[2 * e + 1], send.at[2 * e + 1], recv.at[2 * e + 1], z, sibling)

    def begin(buf, send, recv):
        forward(buf, send, recv, 0).start()
        for e in range(1, min(3, chips)):
            push(buf, send, recv, e).start()

    def chunk_step(q, buf, send, recv, total, then):
        s, slot = q % nv, q % SLOTS
        e = s // 2
        prefetch(q + SLOTS - 1)

        @pl.when((s % 2 == 0) & (s > 0))
        def _():
            push(buf, send, recv, e).wait_recv()
            forward(buf, send, recv, e).start()

            @pl.when(e + 2 < chips)
            def _():
                push(buf, send, recv, e + 2).start()

            @pl.when(e == chips - 1)
            def _():
                then()

        @pl.when(s % 2 == 1)
        def _():
            forward(buf, send, recv, e).wait_recv()

        fetch(t_weight, q).wait()

        @pl.loop(0, width // tile_rows)
        def _(j):
            rows = pl.ds(pl.multiple_of(j * tile_rows, tile_rows), tile_rows)
            total[rows, :] += lax.dot_general(
                wbuf[slot, rows, :], buf[s], (((1,), (1,)), ((), ())), preferred_element_type=jnp.float32
            )

    def finish_sends(buf, send, recv):
        @pl.loop(0, chips)
        def _(e):
            forward(buf, send, recv, e).wait_send()

        @pl.loop(1, chips)
        def _(e):
            push(buf, send, recv, e).wait_send()

    def of_batch(b):
        return hid.at[b], h_send.at[b], h_recv.at[b]

    begin(*of_batch(0))

    pass_student = remote(student, shid.at[0, mine], p_send, p_recv.at[place], end, v)
    pass_targets = remote(targets, tbuf.at[place], t_send, t_recv.at[place], end, v)

    @pl.when(z != end)
    def _():
        pass_student.start()
        pass_targets.start()

    for b in range(1, batches):
        clear(b)

    @pl.when(is_end)
    def _():
        @pl.loop(0, width // block)
        def _(i):
            sacc[block_rows(i), :] = jnp.zeros((block, half), jnp.float32)

    def begin_student():
        @pl.when(is_end)
        def _():
            own_student.wait()
            own_targets.wait()

            @pl.loop(0, half_n)
            def _(j):
                @pl.when(j != place)
                def _():
                    there = pl.ds(pl.multiple_of(j * per, per), per)
                    remote(student, shid.at[0, there], p_send, p_recv.at[j], z, v).wait_recv()
                    remote(targets, tbuf.at[j], t_send, t_recv.at[j], z, v).wait_recv()

            begin(shid, s_send, s_recv)

    def teacher_step(b, s):
        def then():
            @pl.when(b + 1 < batches)
            def _():
                begin(*of_batch(b + 1))

            @pl.when(b + 1 == batches)
            def _():
                begin_student()

        chunk_step(b * nv + s, *of_batch(b), acc.at[b], then)

    def fold(x, reduce):
        return reduce(x.reshape(block // 8, 8, x.shape[1]), axis=0)

    def highest(logits):
        low = jnp.full((8, logits.shape[1]), -jnp.inf, jnp.float32)
        top = lax.fori_loop(
            0, width // block, lambda i, top: jnp.maximum(top, fold(logits[block_rows(i), :], jnp.max)), low
        )
        return jnp.max(top, axis=0, keepdims=True)

    def rows_of(*values):
        row = lax.broadcasted_iota(jnp.int32, (8, values[0].shape[1]), 0)
        packed = jnp.zeros(row.shape, jnp.float32)
        for i, value in enumerate(values):
            packed = jnp.where(row == i, value, packed)
        return packed

    def normalize(b):
        logits = acc.at[b]
        top = highest(logits)

        def exponentials(i, total):
            x = jnp.exp(logits[block_rows(i), :] - top)
            logits[block_rows(i), :] = x
            return total + fold(x, jnp.sum)

        total = lax.fori_loop(0, width // block, exponentials, jnp.zeros((8, 2 * LANES), jnp.float32))
        rows_in[b, 0] = rows_of(top, jnp.sum(total, axis=0, keepdims=True))
        exchange_start(rows_in.at[b], l_send.at[b], l_recv.at[b])

    def exchange_start(buf, send, recv):
        @pl.loop(1, nv)
        def _(d):
            remote(buf.at[0], buf.at[d], send.at[d], recv.at[d], z, (v + d) % nv).start()

    def exchange_wait(buf, send, recv):
        @pl.loop(1, nv)
        def _(d):
            remote(buf.at[0], buf.at[d], send.at[d], recv.at[d], z, (v + d) % nv).wait()

    def merge(buf):
        top = buf[0, 0:1, :]
        for d in range(1, nv):
            top = jnp.maximum(top, buf[d, 0:1, :])
        total = jnp.zeros_like(top)
        for d in range(nv):
            total += buf[d, 1:2, :] * jnp.exp(buf[d, 0:1, :] - top)
        return top + jnp.log(total)

    weights = branch_weight[...]
    log_share = jnp.log(weights / jnp.sum(weights, axis=1, keepdims=True))
    index = lax.broadcasted_iota(jnp.int32, weights.shape, 1)
    chosen = jnp.sum(
        jnp.where(index == z, assignment[...].astype(jnp.float32), 0.0), axis=1, keepdims=True
    )
    own_share = jnp.sum(
        jnp.where(index.astype(jnp.float32) == chosen, log_share, 0.0), axis=1, keepdims=True
    )
    def weigh(b):
        stats = rows_in.at[b]
        exchange_wait(stats, l_send.at[b], l_recv.at[b])
        scale = jnp.exp(stats[0, 0:1, :] - merge(stats) + own_share) * SCALE
        factor[b] = jnp.broadcast_to(scale, (8, 2 * LANES))

    @pl.loop(0, nv)
    def _(s):
        teacher_step(0, s)

    normalize(0)

    def piece_up(c):
        return remote(up_out.at[c], up_in.at[c], up_send.at[c], up_recv.at[c], lax.rem(z + 1, n), v)

    def piece_down(c):
        return remote(down_out.at[c], down_in.at[c], down_send.at[c], down_recv.at[c], lax.rem(z + n - 1, n), v)

    def turn(c, side, order, piece, came, leaves):
        b = c // pieces
        rows = pl.ds(pl.multiple_of(c % pieces * rows_each, rows_each), rows_each)
        lanes = pl.ds(side * LANES, LANES)

        @pl.when(order == 0)
        def _():
            p = acc[b, rows, lanes] * factor[b, :1, lanes]
            p = p * p
            leaves[c] = (p * p).astype(jnp.bfloat16)
            piece(c).start()

        @pl.when(order > 0)
        def _():
            piece(c).wait_recv()
            p = acc[b, rows, lanes] * factor[b, :1, lanes] + lax.rsqrt(lax.rsqrt(came[c].astype(jnp.float32)))

            @pl.when(order < n - 1)
            def _():
                square = p * p
                leaves[c] = (square * square).astype(jnp.bfloat16)
                piece(c).start()

            @pl.when(order == n - 1)
            def _():
                acc[b, rows, lanes] = p

    def find_top():
        s_top[...] = jnp.broadcast_to(highest(sacc), (8, half))

    def compare(b):
        lanes = pl.ds(pl.multiple_of(upper * LANES, LANES), LANES)
        here = pl.ds(b * LANES, LANES)
        top = s_top[:1, here]
        picks = tbuf[0, :1, here]
        for j in range(1, half_n):
            picks = picks + tbuf[j, :1, here]
        picks = picks - v * width
        vocab_row = lax.broadcasted_iota(jnp.int32, (block, LANES), 0)

        def terms(i, sums):
            x = sacc[block_rows(i), here]
            q = acc[b, block_rows(i), lanes]
            hit = jnp.where(vocab_row + i * block == picks, x, 0.0)
            x = x - top
            mixture = jnp.log(jnp.maximum(q, 1e-30)) - LOG_SCALE
            q = q * (1.0 / SCALE)
            new = (jnp.exp(x), hit, q * (mixture - x), q)
            return tuple(old + fold(value, jnp.sum) for old, value in zip(sums, new))

        sums = lax.fori_loop(0, width // block, terms, (jnp.zeros((8, LANES), jnp.float32),) * 4)
        fin_in[0, :, here] = rows_of(top, *(jnp.sum(value, axis=0, keepdims=True) for value in sums))

    busy = pieces - 2
    each = -(-nv // busy)

    @pl.loop(0, batches * pieces + LAG * (n - 1))
    def _(k):
        period, j = k // pieces, k % pieces

        @pl.when((j == 0) & (period < batches))
        def _():
            weigh(period)

        c = k - LAG * z

        @pl.when((c >= 0) & (c < batches * pieces))
        def _():
            turn(c, 1, z, piece_up, up_in, up_out)

        o = n - 1 - z
        d = k - LAG * o

        @pl.when((d >= 0) & (d < batches * pieces))
        def _():
            turn(d, 0, o, piece_down, down_in, down_out)

        @pl.when((period + 1 < batches) & (j < busy))
        def _():
            for u in range(each):
                @pl.when(j * each + u < nv)
                def _():
                    teacher_step(period + 1, j * each + u)

        @pl.when((period + 1 < batches) & (j == busy))
        def _():
            normalize(period + 1)

        @pl.when(is_end & (period + 1 == batches) & (j < busy))
        def _():
            for u in range(each):
                @pl.when(j * each + u < nv)
                def _():
                    chunk_step(batches * nv + j * each + u, shid, s_send, s_recv, sacc, lambda: None)

        @pl.when(is_end & (period + 1 == batches) & (j == busy))
        def _():
            find_top()

        for b in range(batches - 1):
            ready = max(batches * pieces - 1 + b, (b + 1) * pieces + LAG * (n - 1))

            @pl.when(is_end & (k == ready))
            def _():
                compare(b)

    @pl.when(is_end)
    def _():
        compare(batches - 1)
        exchange_start(fin_in, f_send, f_recv)
        exchange_wait(fin_in, f_send, f_recv)
        lse = merge(fin_in)
        hit, cross, mass = (jnp.zeros((1, half), jnp.float32) for _ in range(3))
        for d in range(nv):
            hit += fin_in[d, 2:3, :]
            mass += fin_in[d, 4:5, :]
            cross += fin_in[d, 3:4, :] + fin_in[d, 4:5, :] * (lse - fin_in[d, 0:1, :])
        row = lax.broadcasted_iota(jnp.int32, (8, half), 0)
        res[...] = jnp.where(row == 0, cross / mass - jnp.log(mass), lse - hit)

        def give(j):
            return remote(res, res, r_send.at[j], r_recv, upper * half_n + j, v)

        for act in ("start", "wait_send"):
            @pl.loop(0, half_n)
            def _(j):
                @pl.when(j != place)
                def _():
                    getattr(give(j), act)()

        finish_sends(shid, s_send, s_recv)

    @pl.when(z != end)
    def _():
        remote(res, res, r_send.at[0], r_recv, end, v).wait_recv()
        pass_student.wait_send()
        pass_targets.wait_send()

    out[...] = res[...]
    for b in range(batches):
        finish_sends(*of_batch(b))

    @pl.loop(0, batches * pieces)
    def _(c):
        @pl.when(z < n - 1)
        def _():
            piece_up(c).wait_send()

        @pl.when(z > 0)
        def _():
            piece_down(c).wait_send()


def per_device(
    teacher_hidden,
    teacher_weight,
    student_hidden,
    student_weight,
    branch_weight,
    assignment,
    targets,
):
    n, nv = lax.axis_size("branch"), lax.axis_size("vocab")
    _, tokens, feat = teacher_hidden.shape
    width = teacher_weight.shape[2]
    half, per = tokens // 2, tokens // n
    rows_each = piece_rows(width)
    batches = half // LANES
    moves = batches * (width // rows_each)
    first = lax.axis_index("branch") % (n // 2) * per
    spread = jnp.zeros((8, half), jnp.int32)
    spread = lax.dynamic_update_slice(spread, jnp.broadcast_to(targets[None], (8, per)), (0, first))
    f32, bf16 = jnp.float32, jnp.bfloat16
    dma = pltpu.SemaphoreType.DMA
    anywhere = pl.BlockSpec(memory_space=pl.ANY)
    vmem = pl.BlockSpec(memory_space=pltpu.VMEM)
    result = pl.pallas_call(
        functools.partial(kernel, n, nv),
        out_shape=jax.ShapeDtypeStruct((8, half), f32),
        in_specs=[anywhere, anywhere, anywhere, anywhere, vmem, vmem, vmem],
        out_specs=vmem,
        scratch_shapes=[
            pltpu.VMEM((batches, nv, 2 * LANES, feat), bf16),
            pltpu.VMEM((nv, half, feat), bf16),
            pltpu.VMEM((SLOTS, width, feat), bf16),
            pltpu.VMEM((batches, width, 2 * LANES), f32),
            pltpu.VMEM((width, half), f32),
            pltpu.VMEM((moves, rows_each, LANES), bf16),
            pltpu.VMEM((moves, rows_each, LANES), bf16),
            pltpu.VMEM((moves, rows_each, LANES), bf16),
            pltpu.VMEM((moves, rows_each, LANES), bf16),
            pltpu.VMEM((batches, 8, 2 * LANES), f32),
            pltpu.VMEM((8, half), f32),
            pltpu.VMEM((batches, nv, 8, 2 * LANES), f32),
            pltpu.VMEM((nv, 8, half), f32),
            pltpu.VMEM((n // 2, 8, half), jnp.int32),
            pltpu.VMEM((8, half), f32),
            dma((2 + 2 * batches,)),
            dma((SLOTS,)),
            dma((batches, nv)), dma((batches, nv)),
            dma((nv,)), dma((nv,)),
            dma, dma((n // 2,)),
            dma, dma((n // 2,)),
            dma((moves,)), dma((moves,)),
            dma((moves,)), dma((moves,)),
            dma((batches, nv)), dma((batches, nv)),
            dma((nv,)), dma((nv,)),
            dma((n // 2,)), dma,
        ],
        compiler_params=pltpu.CompilerParams(
            collective_id=0, has_side_effects=True, vmem_limit_bytes=60 * 2**20
        ),
    )(
        teacher_hidden,
        jnp.swapaxes(teacher_weight, 1, 2),
        student_hidden,
        student_weight.T,
        branch_weight[None],
        assignment[None],
        spread,
    )
    mine = lax.dynamic_slice(result, (0, first), (2, per))
    return mine[0], mine[1]


def solution(mesh):
    in_specs = (
        P("branch", None, "vocab"),
        P("branch", None, "vocab"),
        P("branch", "vocab"),
        P(None, "vocab"),
        P(),
        P(),
        P("branch"),
    )
    out_specs = (P("branch"), P("branch"))
    return jax.shard_map(
        per_device, mesh=mesh, in_specs=in_specs, out_specs=out_specs, check_vma=False
    )
```

time: 159 us -> 136 us (0.86)
  Pallas kernels: 155 us -> 132 us
    pallas_call x1, Pallas kernels: 155 us -> 132 us  [per_device(): pl.pallas_call(functools.partial(kernel, n, nv), out_shape=jax.ShapeDtype...]
where the time goes in v3:
time: 136 us
  Pallas kernels  132 us (97%)
  local copies, waits for them, and re-layouts  2.87 us (2%)
    pallas_call x1, Pallas kernels, per_device(): pl.pallas_call(functools.partial(kernel, n, nv), out_shape=jax.ShapeDtype...  132 us

profile of v3, /device:TPU:0, one launch (start us, length us, event | category | flops | bytes accessed | tf_op | source)
XLA Modules:
  0.0 135.9 jit_solution(11392121014588434469)
XLA Ops:
  0.6 0.7 broadcast_in_dim.18
  1.3 0.2 dynamic_update_slice.3.targets
  1.5 0.0 copy-start
  1.5 0.6 copy-done
  2.1 132.3 %shard_map.86 = f32[8,384]{1,0:T(8,128)} custom-call(bf16[1,768,512]{2,1,0:T(8,128)(2,1)} %hidden.1, bf16[1,4000,4096]{2,1,0:T(8,128)(2,1)} %bitcast.6, bf16[192,512]{1,0:T(8,128)(2,1)} %student.1, bf16[4000,4096]{1,0:T(8,128)(2,1)} %bitcast.7, f32[1,4]{1,0:T(1,128)} %bitcast.10, s32[1,4]{1,0:T(1,128)} %bitcast.11, s32[8,384]{1,0:T(8,128)} %copy-done), custom_call_target="tpu_custom_call" | custom-call | tf_op jit(solution)/shard_map/pallas_call | solution.py:474
  134.4 1.4 %fusion = (f32[1,192]{1,0:T(1,128)}, f32[1,192]{1,0:T(1,128)}) fusion(f32[8,384]{1,0:T(8,128)} %shard_map.86, s32[]{:T(128)S(6)} %add.10, s32[]{:T(128)S(6)} %select_n.12), kind=kLoop, calls=%fused_computation.1 | loop fusion | bytes 3080 | tf_op jit(solution)/shard_map/slice | solution.py:520
  (1 shorter events, 0.0 us)
Async XLA Ops:
  1.5 0.6 copy-start

commit v4 on v3

--- a/solution.py
+++ b/solution.py
@@ -13,7 +13,7 @@
 LANES = 128
 PIECES = 10
 BLOCK = 80
-TILE = 800
+TILE = 2000
 SLOTS = 4
 LAG = 2
 
@@ -359,22 +359,31 @@
         def _():
             weigh(period)
 
-        c = k - LAG * z
-
-        @pl.when((c >= 0) & (c < batches * pieces))
-        def _():
-            turn(c, 1, z, piece_up, up_in, up_out)
-
-        o = n - 1 - z
-        d = k - LAG * o
-
-        @pl.when((d >= 0) & (d < batches * pieces))
-        def _():
-            turn(d, 0, o, piece_down, down_in, down_out)
+        ahead = k - (batches - 1) * pieces
+
+        def turns(side, order, *rest):
+            c = k - LAG * order
+
+            @pl.when((c >= 0) & (c < batches * pieces) & ((order > 0) | (ahead <= 0)))
+            def _():
+                turn(c, side, order, *rest)
+
+            @pl.when((order == 0) & (ahead > 0))
+            def _():
+                for u in range(2):
+                    later = (batches - 1) * pieces + 2 * ahead - 1 + u
+
+                    @pl.when(later < batches * pieces)
+                    def _():
+                        turn(later, side, order, *rest)
+
+        turns(1, z, piece_up, up_in, up_out)
+        turns(0, n - 1 - z, piece_down, down_in, down_out)
 
         @pl.when((period + 1 < batches) & (j < busy))
         def _():
-            for u in range(each):
+            @pl.loop(0, each)
+            def _(u):
                 @pl.when(j * each + u < nv)
                 def _():
                     teacher_step(period + 1, j * each + u)
@@ -385,7 +394,8 @@
 
         @pl.when(is_end & (period + 1 == batches) & (j < busy))
         def _():
-            for u in range(each):
+            @pl.loop(0, each)
+            def _(u):
                 @pl.when(j * each + u < nv)
                 def _():
                     chunk_step(batches * nv + j * each + u, shid, s_send, s_recv, sacc, lambda: None)

time: 136 us -> 123 us (0.904)
  Pallas kernels: 132 us -> 120 us
    pallas_call x1, Pallas kernels: 132 us -> 120 us  [per_device(): pl.pallas_call(functools.partial(kernel, n, nv), out_shape=jax.ShapeDtype...]
where the time goes in v4:
time: 123 us
  Pallas kernels  120 us (98%)
  local copies, waits for them, and re-layouts  2.87 us (2%)
    pallas_call x1, Pallas kernels, per_device(): pl.pallas_call(functools.partial(kernel, n, nv), out_shape=jax.ShapeDtype...  120 us

profile of v4, /device:TPU:0, one launch (start us, length us, event | category | flops | bytes accessed | tf_op | source)
XLA Modules:
  0.0 123.1 jit_solution(9550755071060493570)
XLA Ops:
  0.6 0.7 broadcast_in_dim.18
  1.3 0.2 dynamic_update_slice.3.targets
  1.5 0.0 copy-start
  1.5 0.6 copy-done
  2.1 119.6 %shard_map.86 = f32[8,384]{1,0:T(8,128)} custom-call(bf16[1,768,512]{2,1,0:T(8,128)(2,1)} %hidden.1, bf16[1,4000,4096]{2,1,0:T(8,128)(2,1)} %bitcast.6, bf16[192,512]{1,0:T(8,128)(2,1)} %student.1, bf16[4000,4096]{1,0:T(8,128)(2,1)} %bitcast.7, f32[1,4]{1,0:T(1,128)} %bitcast.10, s32[1,4]{1,0:T(1,128)} %bitcast.11, s32[8,384]{1,0:T(8,128)} %copy-done), custom_call_target="tpu_custom_call" | custom-call | tf_op jit(solution)/shard_map/pallas_call | solution.py:484
  121.7 1.4 %fusion = (f32[1,192]{1,0:T(1,128)}, f32[1,192]{1,0:T(1,128)}) fusion(f32[8,384]{1,0:T(8,128)} %shard_map.86, s32[]{:T(128)S(6)} %add.10, s32[]{:T(128)S(6)} %select_n.12), kind=kLoop, calls=%fused_computation.1 | loop fusion | bytes 3080 | tf_op jit(solution)/shard_map/slice | solution.py:530
  (1 shorter events, 0.0 us)
Async XLA Ops:
  1.5 0.6 copy-start
